TPU v7x, 256 devices: a whole 4x4x8 slice. The times are simulated.
256 devices in a mesh: row: 32 (over z, y_hi, core), rep: 8 (over y_lo, x).
Axes of the slice: x: 4, y: 4 (y_hi: 2, y_lo: 2; y = y_hi * 2 + y_lo), z: 8, core: 2. Of those that a mesh axis runs over, the one named last changes fastest.
Arguments:
- features: bfloat16 [32768, 256], P(('row', 'rep')), may hold values from -6 to 6
- weight: bfloat16 [256, 256], replicated, may hold values from -0.375 to 0.375
- tiles: bfloat16 [32, 8, 128, 128, 128], P('row', 'rep'), as said below
- tile_source: int32 [32, 8, 128], P('row', 'rep'), may hold values from 0 to 31, as said below
- tile_target: int32 [32, 8, 128], P('row', 'rep'), may hold values from 0 to 7, as said below
- live_tiles: int32 [32, 8], P('row', 'rep'), may hold values from 16 to 128, as said below
- wanted: int32 [32, 8, 32, 1], P('row', 'rep'), may hold values from 0 to 7
Outputs:
- aggregate: bfloat16 [32768, 256], P(('row', 'rep'))
Inputs may be any that keep to these rules, and one draw needn't show every extreme that they name: `live_tiles`: device (0, 0) holds all 128 slots filled; each count is max(1, 128 // m) for m of 1, 2, 4 or 8. Within one device the pairs (tile_source, tile_target) of its slots are all different. Within one device the pairs (tile_source, tile_target) of its slots are all different. `tiles`: Nonnegative.
All inputs are finite; a program needn't handle non-finite values.
Results may differ from a plain program's by a relative error of at most 0.0049.
Values may be sent and summed in bfloat16 or wider, within the bound.
A program may use at most 128 MiB of HBM per device.

v0:
```python
import jax
import jax.numpy as jnp
from jax import lax
from jax.sharding import PartitionSpec as P

F = 256
BLOCK = 128
MOST = 1
NB_DEV = 8
TILES_DEV = 128


def local(features, weight, tiles, tile_source, tile_target, live_tiles, wanted):
    row_count = lax.axis_size("row")
    hidden = jnp.dot(features, weight, preferred_element_type=jnp.float32).astype(jnp.bfloat16)
    slab = lax.all_gather(hidden, "rep", axis=0, tiled=True)
    blocks = slab.reshape(NB_DEV, BLOCK, F)
    requests = wanted.reshape(row_count, MOST)
    everything = lax.all_gather(blocks, "row", axis=0, tiled=True)
    starts = (jnp.arange(row_count, dtype=jnp.int32) * NB_DEV)[:, None]
    panels = everything[(starts + requests).reshape(-1)]
    chosen = panels[tile_source.reshape(-1)]
    products = jnp.einsum(
        "tij,tjf->tif",
        tiles.reshape(TILES_DEV, BLOCK, BLOCK),
        chosen,
        preferred_element_type=jnp.float32,
    )
    alive = (jnp.arange(TILES_DEV, dtype=jnp.int32) < live_tiles.reshape(())).astype(jnp.float32)
    partial_sum = jax.ops.segment_sum(
        products * alive[:, None, None], tile_target.reshape(-1), num_segments=NB_DEV
    )
    partial_sum = partial_sum.reshape(NB_DEV * BLOCK, F)
    summed = lax.psum_scatter(partial_sum, "rep", scatter_dimension=0, tiled=True)
    return summed.astype(jnp.bfloat16)


def solution(mesh):
    placed = (
        P(("row", "rep"), None),
        P(),
        P("row", "rep", None, None, None),
        P("row", "rep", None),
        P("row", "rep", None),
        P("row", "rep"),
        P("row", "rep", None, None),
    )
    return jax.shard_map(
        local, mesh=mesh, in_specs=placed, out_specs=P(("row", "rep"), None), check_vma=False
    )
```

profile of v0, /device:TPU:1, one launch (start us, length us, event | category | flops | bytes accessed | tf_op | source)
XLA Modules:
  0.0 291.6 jit_solution(9734002400545474758)
XLA Ops:
  6.5 0.0 copy-start
  6.5 0.0 all-gather.2.cloned.1.call-start
  6.5 0.9 copy-done
  7.4 1.0 convolution_convert_fusion
  8.4 26.3 %all_gather.6 = bf16[1024,256]{1,0:T(8,128)(2,1)} all-gather(bf16[128,256]{1,0:T(8,128)(2,1)S(1)} %convolution_convert_fusion), channel_id=1, replica_groups=mesh['row'=32,'rep'=8] {'rep'}, dimensions={0}, use_global_device_ids=true | all-gather | bytes 589824 | tf_op jit(solution)/shard_map/all_gather | solution.py:16
  34.7 0.0 all-gather.2.cloned.1.call-update
  34.8 0.0 reduce-scatter.2.cloned.1.call-start
  35.5 0.7 fusion.1
  36.1 0.7 fusion.2
  36.8 144.5 %all-gather.2.cloned.1.call-done = bf16[256,128,256]{2,1,0:T(8,128)(2,1)} async-done(((bf16[8,128,256]{2,1,0:T(8,128)(2,1)}), bf16[256,128,256]{2,1,0:T(8,128)(2,1)}) %all-gather.2.cloned.1.call-update) | async-done | bytes 16777232 | tf_op jit(solution)/shard_map/all_gather | solution.py:19
  181.3 6.4 %gather_fusion = bf16[32,128,256]{2,1,0:T(8,128)(2,1)S(1)} fusion(bf16[256,128,256]{2,1,0:T(8,128)(2,1)} %all-gather.2.cloned.1.call-done, s32[1024]{0:T(1024)S(1)} %pad_clamp_fusion.1), kind=kCustom, calls=%fused_computation | custom fusion | bytes 4194432 | tf_op jit(solution)/shard_map/gather | solution.py:21
  187.7 6.6 %gather_fusion.1 = bf16[128,128,256]{2,1,0:T(8,128)(2,1)} fusion(bf16[32,128,256]{2,1,0:T(8,128)(2,1)S(1)} %gather_fusion, s32[1024]{0:T(1024)S(1)} %pad_clamp_fusion), kind=kCustom, calls=%fused_computation.1 | custom fusion | bytes 16777728 | tf_op jit(solution)/shard_map/gather | solution.py:22
  194.3 12.9 %multiply_bitcast_fusion = f32[128,128,256]{1,2,0:T(8,128)} fusion(bf16[128,128,256]{2,1,0:T(8,128)(2,1)} %gather_fusion.1, f32[128]{0:T(128)S(1)} %compare_convert_fusion, bf16[1,1,128,128,128]{4,3,2,1,0:T(8,128)(2,1)} %param.9), kind=kOutput, calls=%fused_computation.3 | convolution fusion | flops 1077936128 | bytes 29360640 | tf_op jit(solution)/shard_map/tij,tjf->tif/dot_general | solution.py:23
  207.2 0.0 copy-start.3
  207.2 17.5 %copy.12 = f32[128,128,256]{2,1,0:T(8,128)} copy(f32[128,128,256]{1,2,0:T(8,128)} %multiply_bitcast_fusion) | data formatting | bytes 33554432 | tf_op jit(solution)/shard_map/mul | solution.py:31
  224.7 0.1 broadcast_in_dim.2
  224.8 0.0 copy-done.3
  224.8 0.0 copy-start.1
  224.8 24.2 %scatter_fusion = f32[8,128,256]{2,1,0:T(8,128)S(1)} fusion(f32[8,128,256]{2,1,0:T(8,128)S(1)} %broadcast_in_dim.2, s32[128]{0:T(128)S(1)} %bitcast.25, f32[128,128,256]{2,1,0:T(8,128)} %copy.12), kind=kCustom, calls=%fused_computation.2 | custom fusion | flops 4194304 | bytes 50332160 | tf_op jit(solution)/shard_map/scatter-add | solution.py:30
  249.0 0.0 copy-start.2
  249.0 1.0 copy-done.2
  250.0 0.0 reduce-scatter.2.cloned.1.call-update
  250.0 33.2 %reduce-scatter.2.cloned.1.call-done = f32[128,256]{1,0:T(8,128)} async-done(((f32[1024,256]{1,0:T(8,128)}), f32[128,256]{1,0:T(8,128)}) %reduce-scatter.2.cloned.1.call-update) | async-done | bytes 131088 | tf_op jit(solution)/shard_map/reduce_scatter | solution.py:34
  283.2 1.5 convert_element_type.15
  284.7 0.0 copy-done.1
  (3 shorter events, 0.0 us)
Async XLA Ops:
  6.5 0.9 copy-start
  6.5 174.7 %all-gather.2.cloned.1.call-start = ((), (), s32[]{:S(2)}) async-start(), calls=%async_computation.1 | async-start | bytes 17301504 | tf_op jit(solution)/shard_map/all_gather | solution.py:19
  34.8 248.4 %reduce-scatter.2.cloned.1.call-start = ((), (), s32[]{:S(2)}) async-start(), calls=%async_computation.2 | async-start | bytes 1179648 | tf_op jit(solution)/shard_map/reduce_scatter | solution.py:34
  207.2 17.6 %copy-start.3 = (s32[1,1,128]{2,1,0:T(1,128)S(1)}, s32[1,1,128]{2,1,0:T(1,128)}, u32[]{:S(2)}) copy-start(s32[1,1,128]{2,1,0:T(1,128)} %param.11) | copy-start | bytes 1540
  224.8 59.9 %copy-start.1 = (bf16[256,256]{1,0:T(8,128)(2,1)S(1)}, bf16[256,256]{1,0:T(8,128)(2,1)}, u32[]{:S(2)}) copy-start(bf16[256,256]{1,0:T(8,128)(2,1)} %param.8) | copy-start | bytes 393220
  249.0 1.0 copy-start.2
Sparse Core Ops, SparseCore 0:
  34.9 146.3 all-gather.1
  250.1 33.0 reduce-scatter.1
where the time goes:
time: 296 us; the launch traced here: 292 us
  waiting for transfers between devices  178 us (60%)
  local copies, waits for them, and re-layouts  32.4 us (11%)
  other arithmetic  27.1 us (9%)
  blocking collectives  26.3 us (9%)
  between operations  14.1 us (5%)
  matrix products  13.9 us (5%)
    all_gather x1, waiting for transfers between devices, local(): everything = lax.all_gather(blocks, 'row', axis=0, tiled=True)  144 us
    reduce_scatter x1, waiting for transfers between devices, local(): lax.psum_scatter(partial_sum, 'rep', scatter_dimension=0, tiled=True)  33.2 us
    all_gather x1, blocking collectives, local(): slab = lax.all_gather(hidden, 'rep', axis=0, tiled=True)  26.3 us
    scatter-add x1, other arithmetic, local(): jax.ops.segment_sum(products * alive[:, None, None], tile_target.reshape(...  24.2 us
    mul x1, local copies, waits for them, and re-layouts, local(): products * alive[:, None, None]  17.5 us
    dot_general x1, matrix products, local(): jnp.einsum('tij,tjf->tif', tiles.reshape(TILES_DEV, BLOCK, BLOCK), chosen...  12.9 us
    gather x1, local copies, waits for them, and re-layouts, local(): chosen = panels[tile_source.reshape(-1)]  6.56 us
    gather x1, local copies, waits for them, and re-layouts, local(): panels = everything[(starts + requests).reshape(-1)]  6.45 us
  transfers between devices with their start and end apart: 2, of which 2 were waited for; matrix products, arithmetic and copies ran while one was open for 0% of the time, Pallas kernels for 0%

commit v1 on v0

v1 whole, which is shorter than its diff:
```python
import functools

import jax
import jax.numpy as jnp
from jax import lax
from jax.experimental import pallas as pl
from jax.experimental.pallas import tpu as pltpu
from jax.sharding import PartitionSpec as P

F = 256
BLOCK = 128
NB = 8
TILES = 128
SLABS = 32
GROUP = 4
MESH = pl.DeviceIdType.MESH

OFFSETS = [
    (2, 0, 0), (0, 2, 0), (1, 1, 0), (3, 3, 0),
    (1, 3, 0), (3, 1, 0), (1, 0, 1), (3, 0, 1),
    (0, 1, 1), (0, 3, 1), (0, 0, 1), (1, 0, 0),
    (3, 0, 0), (0, 1, 0), (0, 3, 0), (0, 0, 0),
]
HOME = OFFSETS.index((0, 0, 0))
N_OFF = len(OFFSETS)


def device(x, y, z, c):
    return (z * 4 + (y // 2) * 2 + c, lax.rem(y, 2) * 4 + x)


def owned_slab(x, y, z, c):
    odd = lax.rem(z, 2)
    zs = lax.rem(x + 2 * odd, 4) + 4 * lax.rem(y, 2)
    yh = lax.rem(y // 2 + odd + lax.rem(zs, 2) + 1, 2)
    return zs, yh


def owner_at(zs, yh, c, z):
    odd = lax.rem(z, 2)
    x = lax.rem(lax.rem(zs, 4) + 2 * odd, 4)
    pair = lax.rem(yh + odd + lax.rem(zs, 2) + 1, 2)
    return device(x, 2 * pair + zs // 4, z, c)


def kernel(
    live_ref, features_ref, weight_ref, tiles_ref, source_ref, target_ref, wanted_ref, out_ref,
    feat_v, weight_v, hidden_v, tiles_v, dense_v, slab_v, picked_v, panel_v, total_v, part_v, land_v,
    ask_v, req_v, slot_v, req_s, slot_s,
    load_sem, small_sem, spread_send, spread_recv, ask_send, ask_recv, give_send, give_recv, sum_send, sum_recv,
):
    r, q = lax.axis_index("row"), lax.axis_index("rep")
    z, yh, c = r // 4, lax.rem(r // 2, 2), lax.rem(r, 2)
    yl, x = q // 4, lax.rem(q, 4)
    y = yh * 2 + yl

    loads = [
        pltpu.make_async_copy(features_ref, feat_v, load_sem.at[0]),
        pltpu.make_async_copy(weight_ref, weight_v, load_sem.at[1]),
        pltpu.make_async_copy(tiles_ref.at[0, 0], tiles_v.at[pl.ds(0, TILES)], load_sem.at[2]),
    ]
    for load in loads:
        load.start()

    def owner_of(k, core):
        dx, dy, dz = OFFSETS[k]
        pz = lax.rem(z + dz * (1 - 2 * core) + 8, 8) if dz else z
        return lax.rem(x + dx, 4), lax.rem(y + dy, 4), pz, core

    def asker_of(k, core):
        dx, dy, dz = OFFSETS[k]
        pz = lax.rem(z - dz * (1 - 2 * c) + 8, 8) if dz else z
        return lax.rem(x + 4 - dx, 4), lax.rem(y + 4 - dy, 4), pz, core

    own_z, own_yh = owned_slab(x, y, z, c)
    own = own_z * 4 + own_yh * 2 + c

    barrier = pltpu.get_barrier_semaphore()
    n_signals = 0

    def tell(dev):
        pl.semaphore_signal(barrier, inc=1, device_id=dev, device_id_type=MESH)

    for b in range(NB):
        tell(device(b % 4, 2 * own_yh + b // 4, own_z, c))
    n_signals += NB
    for k in range(N_OFF):
        cores = (1 - c,) if k == HOME else (0, 1)
        for core in cores:
            tell(device(*owner_of(k, core)))
            tell(device(*asker_of(k, core)))
        n_signals += 2 * len(cores)
    for d in range(1, NB):
        tell((r, lax.rem(q + d, NB)))
    n_signals += NB - 1

    loads[0].wait()
    loads[1].wait()
    hidden_v[...] = jnp.dot(feat_v[...], weight_v[...], preferred_element_type=jnp.float32).astype(jnp.bfloat16)
    ask_v[...] = jnp.zeros_like(ask_v)
    ask_v[:, 0:SLABS] = wanted_ref[...]

    pl.semaphore_wait(barrier, n_signals)

    spreads = []
    for dz in (4, 3, 5, 2, 6, 1, 7, 0):
        spread = pltpu.make_async_remote_copy(
            src_ref=hidden_v, dst_ref=slab_v.at[q], send_sem=spread_send.at[dz], recv_sem=spread_recv.at[q],
            device_id=owner_at(z, yh, c, lax.rem(z + dz, 8)), device_id_type=MESH,
        )
        spread.start()
        spreads.append(spread)
    asks = []
    for k in range(N_OFF):
        for core in (1 - c,) if k == HOME else (0, 1):
            ask = pltpu.make_async_remote_copy(
                src_ref=ask_v, dst_ref=req_v.at[2 * k + c], send_sem=ask_send.at[2 * k + core],
                recv_sem=ask_recv.at[2 * k + c], device_id=device(*owner_of(k, core)), device_id_type=MESH,
            )
            ask.start()
            asks.append(ask)
    mine = pltpu.make_async_copy(ask_v, req_v.at[2 * HOME + c], small_sem.at[0])
    mine.start()

    t_row = lax.broadcasted_iota(jnp.int32, (1, TILES), 1)
    key = jnp.where(t_row < live_ref[0, 0], target_ref[...] * SLABS + source_ref[...], -1)
    here = lax.broadcasted_iota(jnp.int32, (TILES, TILES), 0) == lax.broadcasted_iota(jnp.int32, (TILES, TILES), 1)
    column = jnp.sum(jnp.where(here, jnp.broadcast_to(key, (TILES, TILES)), 0), axis=1, keepdims=True)
    pair = lax.broadcasted_iota(jnp.int32, (TILES, NB * SLABS), 1)
    slot = lax.broadcasted_iota(jnp.int32, (TILES, NB * SLABS), 0)
    found = jnp.where(jnp.broadcast_to(column, (TILES, NB * SLABS)) == pair, slot - TILES, 0)
    slot_v[...] = jnp.sum(found, axis=0, keepdims=True) + TILES
    to_scalar = pltpu.make_async_copy(slot_v, slot_s, small_sem.at[1])
    to_scalar.start()
    tiles_v[TILES] = jnp.zeros((BLOCK, BLOCK), jnp.bfloat16)
    loads[2].wait()
    to_scalar.wait()

    def place(k):
        for core in (0, 1):
            px, py, pz, _ = owner_of(k, core)
            sz, syh = owned_slab(px, py, pz, core)
            s = sz * 4 + syh * 2 + core
            for b in range(NB):
                t = slot_s[0, b * SLABS + s]
                at = (k % GROUP) * 2 * BLOCK + core * BLOCK
                dense_v[k // GROUP, b * BLOCK : (b + 1) * BLOCK, at : at + BLOCK] = tiles_v[t]

    for k in range(N_OFF):
        place(k)

    mine.wait()
    for k in range(N_OFF):
        for core in (1 - c,) if k == HOME else (0, 1):
            pltpu.make_async_remote_copy(
                src_ref=ask_v, dst_ref=req_v.at[2 * k + core], send_sem=ask_send.at[2 * k + core],
                recv_sem=ask_recv.at[2 * k + core], device_id=device(*asker_of(k, core)), device_id_type=MESH,
            ).wait_recv()
    to_scalar = pltpu.make_async_copy(req_v, req_s, small_sem.at[2])
    to_scalar.start()
    to_scalar.wait()

    for b in range(NB):
        pltpu.make_async_remote_copy(
            src_ref=hidden_v, dst_ref=slab_v.at[b], send_sem=spread_send.at[b], recv_sem=spread_recv.at[b],
            device_id=device(b % 4, 2 * own_yh + b // 4, own_z, c), device_id_type=MESH,
        ).wait_recv()

    gives = []
    for k in range(N_OFF):
        for core in (1 - c,) if k == HOME else (0, 1):
            index = 2 * k + core
            picked_v[index] = slab_v[req_s[index, 0, own]]
            give = pltpu.make_async_remote_copy(
                src_ref=picked_v.at[index], dst_ref=panel_v.at[k, c], send_sem=give_send.at[index],
                recv_sem=give_recv.at[2 * k + c], device_id=device(*asker_of(k, core)), device_id_type=MESH,
            )
            give.start()
            gives.append(give)
    panel_v[HOME, c] = slab_v[req_s[2 * HOME + c, 0, own]]

    def arrive(g):
        for k in range(g * GROUP, (g + 1) * GROUP):
            for core in (1 - c,) if k == HOME else (0, 1):
                pltpu.make_async_remote_copy(
                    src_ref=picked_v.at[0], dst_ref=panel_v.at[k, core], send_sem=give_send.at[2 * k + core],
                    recv_sem=give_recv.at[2 * k + core], device_id=device(*owner_of(k, core)), device_id_type=MESH,
                ).wait_recv()

    def panels(g):
        return panel_v[g * GROUP : (g + 1) * GROUP].reshape(2 * GROUP * BLOCK, F)

    ROWS = 256
    last = N_OFF // GROUP - 1
    for g in range(last):
        arrive(g)

        @pl.loop(0, NB * BLOCK // ROWS)
        def _(i):
            at = pl.ds(pl.multiple_of(i * ROWS, ROWS), ROWS)
            term = jnp.dot(dense_v[g, at, :], panels(g), preferred_element_type=jnp.float32)
            if g == 0:
                total_v[at, :] = term
            else:
                total_v[at, :] += term

    arrive(last)
    sums = []
    for d in range(1, NB + 1):
        b = lax.rem(q + d, NB)
        at = pl.ds(pl.multiple_of(b * BLOCK, BLOCK), BLOCK)
        full = total_v[at, :] + jnp.dot(dense_v[last, at, :], panels(last), preferred_element_type=jnp.float32)
        if d < NB:
            part_v[d] = full.astype(jnp.bfloat16)
            part = pltpu.make_async_remote_copy(
                src_ref=part_v.at[d], dst_ref=land_v.at[d], send_sem=sum_send.at[d], recv_sem=sum_recv.at[d],
                device_id=(r, b), device_id_type=MESH,
            )
            part.start()
            sums.append(part)
        else:
            total_v[0:BLOCK, :] = full
    for part in sums:
        part.wait_recv()
    result = total_v[0:BLOCK, :]
    for d in range(1, NB):
        result += land_v[d].astype(jnp.float32)
    out_ref[...] = result.astype(jnp.bfloat16)
    for copy in spreads + asks + gives + sums:
        copy.wait_send()


def local(features, weight, tiles, tile_source, tile_target, live_tiles, wanted):
    vmem = pl.BlockSpec(memory_space=pltpu.VMEM)
    hbm = pl.BlockSpec(memory_space=pl.ANY)
    smem = pl.BlockSpec(memory_space=pltpu.SMEM)
    dma = pltpu.SemaphoreType.DMA
    bf16, f32, i32 = jnp.bfloat16, jnp.float32, jnp.int32
    return pl.pallas_call(
        kernel,
        out_shape=jax.ShapeDtypeStruct((BLOCK, F), bf16),
        in_specs=[smem, hbm, hbm, hbm, vmem, vmem, vmem],
        out_specs=vmem,
        scratch_shapes=[
            pltpu.VMEM((BLOCK, F), bf16),
            pltpu.VMEM((F, F), bf16),
            pltpu.VMEM((BLOCK, F), bf16),
            pltpu.VMEM((TILES + 1, BLOCK, BLOCK), bf16),
            pltpu.VMEM((N_OFF // GROUP, NB * BLOCK, 2 * GROUP * BLOCK), bf16),
            pltpu.VMEM((NB, BLOCK, F), bf16),
            pltpu.VMEM((2 * N_OFF, BLOCK, F), bf16),
            pltpu.VMEM((N_OFF, 2, BLOCK, F), bf16),
            pltpu.VMEM((NB * BLOCK, F), f32),
            pltpu.VMEM((NB, BLOCK, F), bf16),
            pltpu.VMEM((NB, BLOCK, F), bf16),
            pltpu.VMEM((1, 128), i32),
            pltpu.VMEM((2 * N_OFF, 1, 128), i32),
            pltpu.VMEM((1, NB * SLABS), i32),
            pltpu.SMEM((2 * N_OFF, 1, 128), i32),
            pltpu.SMEM((1, NB * SLABS), i32),
            dma((3,)), dma((3,)),
            dma((NB,)), dma((NB,)),
            dma((2 * N_OFF,)), dma((2 * N_OFF,)),
            dma((2 * N_OFF,)), dma((2 * N_OFF,)),
            dma((NB,)), dma((NB,)),
        ],
        compiler_params=pltpu.CompilerParams(
            collective_id=0, has_side_effects=True, vmem_limit_bytes=48 << 20
        ),
    )(
        live_tiles, features, weight, tiles,
        tile_source.reshape(1, TILES), tile_target.reshape(1, TILES), wanted.reshape(1, SLABS),
    )


def solution(mesh):
    placed = (
        P(("row", "rep"), None),
        P(),
        P("row", "rep", None, None, None),
        P("row", "rep", None),
        P("row", "rep", None),
        P("row", "rep"),
        P("row", "rep", None, None),
    )
    return jax.shard_map(
        local, mesh=mesh, in_specs=placed, out_specs=P(("row", "rep"), None), check_vma=False
    )
```

time: 296 us -> 66.5 us (0.22); the launches traced: 292 us -> 66.3 us
  waiting for transfers between devices: 178 us -> 0 us
  Pallas kernels: 0 us -> 59.1 us
  other arithmetic: 27.1 us -> 0 us
  blocking collectives: 26.3 us -> 0 us
  local copies, waits for them, and re-layouts: 32.4 us -> 6.52 us
  matrix products: 13.9 us -> 0 us
  between operations: 14.1 us -> 0.67 us
    all_gather x1 -> x0, waiting for transfers between devices: 144 us -> none  [local(): everything = lax.all_gather(blocks, 'row', axis=0, tiled=True)]
    pallas_call x0 -> x1, Pallas kernels: none -> 59.1 us  [local(): pl.pallas_call(kernel, out_shape=jax.ShapeDtypeStruct((BLOCK, F), bf16),...]
    reduce_scatter x1 -> x0, waiting for transfers between devices: 33.2 us -> none  [local(): lax.psum_scatter(partial_sum, 'rep', scatter_dimension=0, tiled=True)]
    all_gather x1 -> x0, blocking collectives: 26.3 us -> none  [local(): slab = lax.all_gather(hidden, 'rep', axis=0, tiled=True)]
    scatter-add x1 -> x0, other arithmetic: 24.2 us -> none  [local(): jax.ops.segment_sum(products * alive[:, None, None], tile_target.reshape(...]
    mul x1 -> x0, local copies, waits for them, and re-layouts: 17.5 us -> none  [local(): products * alive[:, None, None]]
    dot_general x2 -> x0, matrix products: 13.9 us -> none  [the longest x1 12.9 us: local(): jnp.einsum('tij,tjf->tif', tiles.reshape(TILES_DEV, BLOCK, BLOCK), chosen...]
    gather x2 -> x0, local copies, waits for them, and re-layouts: 13 us -> none  [the longest x1 6.56 us: local(): chosen = panels[tile_source.reshape(-1)]]
  transfers between devices with their start and end apart: 2 -> 0, of which waited for: 2 -> 0; matrix products, arithmetic and copies ran while one was open for 0% -> 0% of each run, Pallas kernels for 0% -> 0%
where the time goes in v1:
time: 66.5 us; the launch traced here: 66.3 us
  Pallas kernels  59.1 us (89%)
  local copies, waits for them, and re-layouts  6.52 us (10%)
  between operations  0.67 us (1%)
    pallas_call x1, Pallas kernels, local(): pl.pallas_call(kernel, out_shape=jax.ShapeDtypeStruct((BLOCK, F), bf16),...  59.1 us
    unnamed x13, local copies, waits for them, and re-layouts  6.52 us

profile of v1, /device:TPU:1, one launch (start us, length us, event | category | flops | bytes accessed | tf_op | source)
XLA Modules:
  0.0 66.3 jit_solution(3137747510025398730)
XLA Ops:
  0.7 0.0 copy-start
  0.7 2.2 %copy-done = bf16[1,1,128,128,128]{4,3,2,1,0:T(8,128)(2,1)S(1)} copy-done((bf16[1,1,128,128,128]{4,3,2,1,0:T(8,128)(2,1)S(1)}, bf16[1,1,128,128,128]{4,3,2,1,0:T(8,128)(2,1)}, u32[]{:S(2)}) %copy-start) | copy-done | bytes 4194328
  2.8 0.0 copy-start.1
  2.8 0.9 %copy-done.1 = bf16[256,256]{1,0:T(8,128)(2,1)S(1)} copy-done((bf16[256,256]{1,0:T(8,128)(2,1)S(1)}, bf16[256,256]{1,0:T(8,128)(2,1)}, u32[]{:S(2)}) %copy-start.1) | copy-done | bytes 131096
  3.7 0.0 copy-start.2
  3.7 0.8 %copy-done.2 = bf16[128,256]{1,0:T(8,128)(2,1)S(1)} copy-done((bf16[128,256]{1,0:T(8,128)(2,1)S(1)}, bf16[128,256]{1,0:T(8,128)(2,1)}, u32[]{:S(2)}) %copy-start.2) | copy-done | bytes 65560
  4.6 0.0 copy-start.3
  4.6 0.7 copy-done.3
  5.2 0.0 copy-start.4
  5.2 0.7 copy-done.4
  5.9 0.0 copy-start.5
  5.9 0.7 copy-done.5
  6.6 59.1 %shard_map.73 = bf16[128,256]{1,0:T(8,128)(2,1)S(1)} custom-call(s32[1,1]{1,0:T(1,128)S(6)} %copy.9.live_ref, bf16[128,256]{1,0:T(8,128)(2,1)S(1)} %copy-done.2, bf16[256,256]{1,0:T(8,128)(2,1)S(1)} %copy-done.1, bf16[1,1,128,128,128]{4,3,2,1,0:T(8,128)(2,1)S(1)} %copy-done, s32[1,128]{1,0:T(1,128)S(1)} %bitcast.3, s32[1,128]{1,0:T(1,128)S(1)} %bitcast.4, ...), custom_call_target="tpu_custom_call" | custom-call | tf_op jit(solution)/shard_map/pallas_call | solution.py:239
  65.7 0.6 copy.10
Async XLA Ops:
  0.7 2.2 %copy-start = (bf16[1,1,128,128,128]{4,3,2,1,0:T(8,128)(2,1)S(1)}, bf16[1,1,128,128,128]{4,3,2,1,0:T(8,128)(2,1)}, u32[]{:S(2)}) copy-start(bf16[1,1,128,128,128]{4,3,2,1,0:T(8,128)(2,1)} %tiles_ref.1) | copy-start | bytes 12582916
  2.8 0.9 %copy-start.1 = (bf16[256,256]{1,0:T(8,128)(2,1)S(1)}, bf16[256,256]{1,0:T(8,128)(2,1)}, u32[]{:S(2)}) copy-start(bf16[256,256]{1,0:T(8,128)(2,1)} %weight_ref.1) | copy-start | bytes 393220
  3.7 0.8 %copy-start.2 = (bf16[128,256]{1,0:T(8,128)(2,1)S(1)}, bf16[128,256]{1,0:T(8,128)(2,1)}, u32[]{:S(2)}) copy-start(bf16[128,256]{1,0:T(8,128)(2,1)} %features_ref.1) | copy-start | bytes 196612
  4.6 0.7 copy-start.3
  5.2 0.7 copy-start.4
  5.9 0.7 copy-start.5

commit v2 on v1

--- a/solution.py
+++ b/solution.py
@@ -46,7 +46,7 @@
 def kernel(
     live_ref, features_ref, weight_ref, tiles_ref, source_ref, target_ref, wanted_ref, out_ref,
     feat_v, weight_v, hidden_v, tiles_v, dense_v, slab_v, picked_v, panel_v, total_v, part_v, land_v,
-    ask_v, req_v, slot_v, req_s, slot_s,
+    source_v, target_v, wanted_v, ask_v, req_v, slot_v, req_s, slot_s,
     load_sem, small_sem, spread_send, spread_recv, ask_send, ask_recv, give_send, give_recv, sum_send, sum_recv,
 ):
     r, q = lax.axis_index("row"), lax.axis_index("rep")
@@ -57,7 +57,10 @@
     loads = [
         pltpu.make_async_copy(features_ref, feat_v, load_sem.at[0]),
         pltpu.make_async_copy(weight_ref, weight_v, load_sem.at[1]),
-        pltpu.make_async_copy(tiles_ref.at[0, 0], tiles_v.at[pl.ds(0, TILES)], load_sem.at[2]),
+        pltpu.make_async_copy(wanted_ref, wanted_v, load_sem.at[2]),
+        pltpu.make_async_copy(source_ref, source_v, load_sem.at[3]),
+        pltpu.make_async_copy(target_ref, target_v, load_sem.at[4]),
+        pltpu.make_async_copy(tiles_ref.at[0, 0], tiles_v.at[pl.ds(0, TILES)], load_sem.at[5]),
     ]
     for load in loads:
         load.start()
@@ -87,23 +90,20 @@
     for k in range(N_OFF):
         cores = (1 - c,) if k == HOME else (0, 1)
         for core in cores:
-            tell(device(*owner_of(k, core)))
             tell(device(*asker_of(k, core)))
-        n_signals += 2 * len(cores)
-    for d in range(1, NB):
-        tell((r, lax.rem(q + d, NB)))
-    n_signals += NB - 1
+        n_signals += len(cores)
 
     loads[0].wait()
     loads[1].wait()
     hidden_v[...] = jnp.dot(feat_v[...], weight_v[...], preferred_element_type=jnp.float32).astype(jnp.bfloat16)
     ask_v[...] = jnp.zeros_like(ask_v)
-    ask_v[:, 0:SLABS] = wanted_ref[...]
+    loads[2].wait()
+    ask_v[:, 0:SLABS] = wanted_v[...]
 
     pl.semaphore_wait(barrier, n_signals)
 
     spreads = []
-    for dz in (4, 3, 5, 2, 6, 1, 7, 0):
+    for dz in (0, 1, 7, 2, 6, 3, 5, 4):
         spread = pltpu.make_async_remote_copy(
             src_ref=hidden_v, dst_ref=slab_v.at[q], send_sem=spread_send.at[dz], recv_sem=spread_recv.at[q],
             device_id=owner_at(z, yh, c, lax.rem(z + dz, 8)), device_id_type=MESH,
@@ -122,8 +122,10 @@
     mine = pltpu.make_async_copy(ask_v, req_v.at[2 * HOME + c], small_sem.at[0])
     mine.start()
 
+    loads[3].wait()
+    loads[4].wait()
     t_row = lax.broadcasted_iota(jnp.int32, (1, TILES), 1)
-    key = jnp.where(t_row < live_ref[0, 0], target_ref[...] * SLABS + source_ref[...], -1)
+    key = jnp.where(t_row < live_ref[0, 0], target_v[...] * SLABS + source_v[...], -1)
     here = lax.broadcasted_iota(jnp.int32, (TILES, TILES), 0) == lax.broadcasted_iota(jnp.int32, (TILES, TILES), 1)
     column = jnp.sum(jnp.where(here, jnp.broadcast_to(key, (TILES, TILES)), 0), axis=1, keepdims=True)
     pair = lax.broadcasted_iota(jnp.int32, (TILES, NB * SLABS), 1)
@@ -133,7 +135,7 @@
     to_scalar = pltpu.make_async_copy(slot_v, slot_s, small_sem.at[1])
     to_scalar.start()
     tiles_v[TILES] = jnp.zeros((BLOCK, BLOCK), jnp.bfloat16)
-    loads[2].wait()
+    loads[5].wait()
     to_scalar.wait()
 
     def place(k):
@@ -239,7 +241,7 @@
     return pl.pallas_call(
         kernel,
         out_shape=jax.ShapeDtypeStruct((BLOCK, F), bf16),
-        in_specs=[smem, hbm, hbm, hbm, vmem, vmem, vmem],
+        in_specs=[smem, hbm, hbm, hbm, hbm, hbm, hbm],
         out_specs=vmem,
         scratch_shapes=[
             pltpu.VMEM((BLOCK, F), bf16),
@@ -253,19 +255,22 @@
             pltpu.VMEM((NB * BLOCK, F), f32),
             pltpu.VMEM((NB, BLOCK, F), bf16),
             pltpu.VMEM((NB, BLOCK, F), bf16),
+            pltpu.VMEM((1, TILES), i32),
+            pltpu.VMEM((1, TILES), i32),
+            pltpu.VMEM((1, SLABS), i32),
             pltpu.VMEM((1, 128), i32),
             pltpu.VMEM((2 * N_OFF, 1, 128), i32),
             pltpu.VMEM((1, NB * SLABS), i32),
             pltpu.SMEM((2 * N_OFF, 1, 128), i32),
             pltpu.SMEM((1, NB * SLABS), i32),
-            dma((3,)), dma((3,)),
+            dma((6,)), dma((3,)),
             dma((NB,)), dma((NB,)),
             dma((2 * N_OFF,)), dma((2 * N_OFF,)),
             dma((2 * N_OFF,)), dma((2 * N_OFF,)),
             dma((NB,)), dma((NB,)),
         ],
         compiler_params=pltpu.CompilerParams(
-            collective_id=0, has_side_effects=True, vmem_limit_bytes=48 << 20
+            collective_id=0, has_side_effects=True, vmem_limit_bytes=63 << 20
         ),
     )(
         live_tiles, features, weight, tiles,

time: 66.5 us -> 58.8 us (0.88)
  local copies, waits for them, and re-layouts: 6.52 us -> 1.47 us
  Pallas kernels: 59.1 us -> 55.9 us
    unnamed x13 -> x1, local copies, waits for them, and re-layouts: 6.52 us -> 1.47 us
    pallas_call x1, Pallas kernels: 59.1 us -> 55.9 us  [local(): pl.pallas_call(kernel, out_shape=jax.ShapeDtypeStruct((BLOCK, F), bf16),...]
where the time goes in v2:
time: 58.8 us; the launch traced here: 58 us
  Pallas kernels  55.9 us (95%)
  local copies, waits for them, and re-layouts  1.47 us (2%)
  between operations  0.66 us (1%)
    pallas_call x1, Pallas kernels, local(): pl.pallas_call(kernel, out_shape=jax.ShapeDtypeStruct((BLOCK, F), bf16),...  55.9 us
    unnamed x1, local copies, waits for them, and re-layouts  1.47 us

profile of v2, /device:TPU:1, one launch (start us, length us, event | category | flops | bytes accessed | tf_op | source)
XLA Modules:
  0.0 58.0 jit_solution(15310553172605889769)
XLA Ops:
  0.7 55.9 %shard_map.73 = bf16[128,256]{1,0:T(8,128)(2,1)} custom-call(s32[1,1]{1,0:T(1,128)S(6)} %copy.9.live_ref, bf16[128,256]{1,0:T(8,128)(2,1)} %features_ref.1, bf16[256,256]{1,0:T(8,128)(2,1)} %weight_ref.1, bf16[1,1,128,128,128]{4,3,2,1,0:T(8,128)(2,1)} %tiles_ref.1, s32[1,128]{1,0:T(1,128)} %bitcast.3, s32[1,128]{1,0:T(1,128)} %bitcast.4, s32[1,32]{1,0:T(1,128)} %bitcast.5), custom_call_target="tpu_custom_call" | custom-call | tf_op jit(solution)/shard_map/pallas_call | solution.py:241
  56.6 1.5 %copy.10 = bf16[128,256]{1,0:T(8,128)(2,1)} copy(bf16[128,256]{1,0:T(8,128)(2,1)} %shard_map.73) | data formatting | bytes 131072

commit v3 on v2

--- a/solution.py
+++ b/solution.py
@@ -23,6 +23,8 @@
 ]
 HOME = OFFSETS.index((0, 0, 0))
 N_OFF = len(OFFSETS)
+PARTS = 2
+WIDE = F // PARTS
 
 
 def device(x, y, z, c):
@@ -45,10 +47,11 @@
 
 def kernel(
     live_ref, features_ref, weight_ref, tiles_ref, source_ref, target_ref, wanted_ref, out_ref,
-    feat_v, weight_v, hidden_v, tiles_v, dense_v, slab_v, picked_v, panel_v, total_v, part_v, land_v,
+    feat_v, weight_v, hidden_v, tiles_v, dense_v, slab_0_v, slab_1_v, picked_v, panel_v, total_v, rest_v, part_v, land_v,
     source_v, target_v, wanted_v, ask_v, req_v, slot_v, req_s, slot_s,
     load_sem, small_sem, spread_send, spread_recv, ask_send, ask_recv, give_send, give_recv, sum_send, sum_recv,
 ):
+    slabs_v = (slab_0_v, slab_1_v)
     r, q = lax.axis_index("row"), lax.axis_index("rep")
     z, yh, c = r // 4, lax.rem(r // 2, 2), lax.rem(r, 2)
     yl, x = q // 4, lax.rem(q, 4)
@@ -95,7 +98,9 @@
 
     loads[0].wait()
     loads[1].wait()
-    hidden_v[...] = jnp.dot(feat_v[...], weight_v[...], preferred_element_type=jnp.float32).astype(jnp.bfloat16)
+    hidden = jnp.dot(feat_v[...], weight_v[...], preferred_element_type=jnp.float32).astype(jnp.bfloat16)
+    for h in range(PARTS):
+        hidden_v[h] = hidden[:, h * WIDE : (h + 1) * WIDE]
     ask_v[...] = jnp.zeros_like(ask_v)
     loads[2].wait()
     ask_v[:, 0:SLABS] = wanted_v[...]
@@ -103,13 +108,17 @@
     pl.semaphore_wait(barrier, n_signals)
 
     spreads = []
-    for dz in (0, 1, 7, 2, 6, 3, 5, 4):
-        spread = pltpu.make_async_remote_copy(
-            src_ref=hidden_v, dst_ref=slab_v.at[q], send_sem=spread_send.at[dz], recv_sem=spread_recv.at[q],
-            device_id=owner_at(z, yh, c, lax.rem(z + dz, 8)), device_id_type=MESH,
-        )
-        spread.start()
-        spreads.append(spread)
+
+    def spread_part(h):
+        for dz in (0, 1, 7, 2, 6, 3, 5, 4):
+            spread = pltpu.make_async_remote_copy(
+                src_ref=hidden_v.at[h], dst_ref=slabs_v[h].at[q], send_sem=spread_send.at[h, dz], recv_sem=spread_recv.at[h, q],
+                device_id=owner_at(z, yh, c, lax.rem(z + dz, 8)), device_id_type=MESH,
+            )
+            spread.start()
+            spreads.append(spread)
+
+    spread_part(0)
     asks = []
     for k in range(N_OFF):
         for core in (1 - c,) if k == HOME else (0, 1):
@@ -119,6 +128,8 @@
             )
             ask.start()
             asks.append(ask)
+    for h in range(1, PARTS):
+        spread_part(h)
     mine = pltpu.make_async_copy(ask_v, req_v.at[2 * HOME + c], small_sem.at[0])
     mine.start()
 
@@ -143,10 +154,12 @@
             px, py, pz, _ = owner_of(k, core)
             sz, syh = owned_slab(px, py, pz, core)
             s = sz * 4 + syh * 2 + core
-            for b in range(NB):
-                t = slot_s[0, b * SLABS + s]
-                at = (k % GROUP) * 2 * BLOCK + core * BLOCK
-                dense_v[k // GROUP, b * BLOCK : (b + 1) * BLOCK, at : at + BLOCK] = tiles_v[t]
+            at = (k % GROUP) * 2 * BLOCK + core * BLOCK
+
+            @pl.loop(0, NB)
+            def _(b):
+                rows = pl.ds(pl.multiple_of(b * BLOCK, BLOCK), BLOCK)
+                dense_v[k // GROUP, rows, at : at + BLOCK] = tiles_v[slot_s[0, b * SLABS + s]]
 
     for k in range(N_OFF):
         place(k)
@@ -162,79 +175,79 @@
     to_scalar.start()
     to_scalar.wait()
 
-    for b in range(NB):
-        pltpu.make_async_remote_copy(
-            src_ref=hidden_v, dst_ref=slab_v.at[b], send_sem=spread_send.at[b], recv_sem=spread_recv.at[b],
-            device_id=device(b % 4, 2 * own_yh + b // 4, own_z, c), device_id_type=MESH,
-        ).wait_recv()
-
     gives = []
-    for k in range(N_OFF):
-        for core in (1 - c,) if k == HOME else (0, 1):
-            index = 2 * k + core
-            picked_v[index] = slab_v[req_s[index, 0, own]]
-            give = pltpu.make_async_remote_copy(
-                src_ref=picked_v.at[index], dst_ref=panel_v.at[k, c], send_sem=give_send.at[index],
-                recv_sem=give_recv.at[2 * k + c], device_id=device(*asker_of(k, core)), device_id_type=MESH,
-            )
-            give.start()
-            gives.append(give)
-    panel_v[HOME, c] = slab_v[req_s[2 * HOME + c, 0, own]]
-
-    def arrive(g):
+    for h in range(PARTS):
+        for b in range(NB):
+            pltpu.make_async_remote_copy(
+                src_ref=hidden_v.at[h], dst_ref=slabs_v[h].at[b], send_sem=spread_send.at[h, b], recv_sem=spread_recv.at[h, b],
+                device_id=device(b % 4, 2 * own_yh + b // 4, own_z, c), device_id_type=MESH,
+            ).wait_recv()
+        for k in range(N_OFF):
+            for core in (1 - c,) if k == HOME else (0, 1):
+                index = 2 * k + core
+                picked_v[h, index] = slabs_v[h][req_s[index, 0, own]]
+                give = pltpu.make_async_remote_copy(
+                    src_ref=picked_v.at[h, index], dst_ref=panel_v.at[h, k, c], send_sem=give_send.at[h, index],
+                    recv_sem=give_recv.at[h, 2 * k + c], device_id=device(*asker_of(k, core)), device_id_type=MESH,
+                )
+                give.start()
+                gives.append(give)
+        panel_v[h, HOME, c] = slabs_v[h][req_s[2 * HOME + c, 0, own]]
+
+    def arrive(h, g):
         for k in range(g * GROUP, (g + 1) * GROUP):
             for core in (1 - c,) if k == HOME else (0, 1):
                 pltpu.make_async_remote_copy(
-                    src_ref=picked_v.at[0], dst_ref=panel_v.at[k, core], send_sem=give_send.at[2 * k + core],
-                    recv_sem=give_recv.at[2 * k + core], device_id=device(*owner_of(k, core)), device_id_type=MESH,
+                    src_ref=picked_v.at[h, 0], dst_ref=panel_v.at[h, k, core], send_sem=give_send.at[h, 2 * k + core],
+                    recv_sem=give_recv.at[h, 2 * k + core], device_id=device(*owner_of(k, core)), device_id_type=MESH,
                 ).wait_recv()
 
-    def panels(g):
-        return panel_v[g * GROUP : (g + 1) * GROUP].reshape(2 * GROUP * BLOCK, F)
+    def panels(h, g):
+        return panel_v[h, g * GROUP : (g + 1) * GROUP].reshape(2 * GROUP * BLOCK, WIDE)
 
     ROWS = 256
     last = N_OFF // GROUP - 1
-    for g in range(last):
-        arrive(g)
-
-        @pl.loop(0, NB * BLOCK // ROWS)
-        def _(i):
-            at = pl.ds(pl.multiple_of(i * ROWS, ROWS), ROWS)
-            term = jnp.dot(dense_v[g, at, :], panels(g), preferred_element_type=jnp.float32)
-            if g == 0:
-                total_v[at, :] = term
+    sums = []
+    for h in range(PARTS):
+        for g in range(last):
+            arrive(h, g)
+
+            @pl.loop(0, NB * BLOCK // ROWS)
+            def _(i):
+                at = pl.ds(pl.multiple_of(i * ROWS, ROWS), ROWS)
+                term = jnp.dot(dense_v[g, at, :], panels(h, g), preferred_element_type=jnp.float32)
+                if g == 0:
+                    total_v[at, :] = term
+                else:
+                    total_v[at, :] += term
+
+        arrive(h, last)
+        for d in range(1, NB + 1):
+            b = lax.rem(q + d, NB)
+            at = pl.ds(pl.multiple_of(b * BLOCK, BLOCK), BLOCK)
+            full = total_v[at, :] + jnp.dot(dense_v[last, at, :], panels(h, last), preferred_element_type=jnp.float32)
+            if d < NB:
+                part_v[h, d] = full.astype(jnp.bfloat16)
+                part = pltpu.make_async_remote_copy(
+                    src_ref=part_v.at[h, d], dst_ref=land_v.at[h, d], send_sem=sum_send.at[h, d], recv_sem=sum_recv.at[h, d],
+                    device_id=(r, b), device_id_type=MESH,
+                )
+                part.start()
+                sums.append((h, d, part))
             else:
-                total_v[at, :] += term
-
-    arrive(last)
-    sums = []
-    for d in range(1, NB + 1):
-        b = lax.rem(q + d, NB)
-        at = pl.ds(pl.multiple_of(b * BLOCK, BLOCK), BLOCK)
-        full = total_v[at, :] + jnp.dot(dense_v[last, at, :], panels(last), preferred_element_type=jnp.float32)
-        if d < NB:
-            part_v[d] = full.astype(jnp.bfloat16)
-            part = pltpu.make_async_remote_copy(
-                src_ref=part_v.at[d], dst_ref=land_v.at[d], send_sem=sum_send.at[d], recv_sem=sum_recv.at[d],
-                device_id=(r, b), device_id_type=MESH,
-            )
-            part.start()
-            sums.append(part)
-        else:
-            total_v[0:BLOCK, :] = full
-    for part in sums:
+                rest_v[h] = full
+    for h, d, part in sums:
         part.wait_recv()
-    result = total_v[0:BLOCK, :]
-    for d in range(1, NB):
-        result += land_v[d].astype(jnp.float32)
-    out_ref[...] = result.astype(jnp.bfloat16)
-    for copy in spreads + asks + gives + sums:
+        rest_v[h] += land_v[h, d].astype(jnp.float32)
+    for h in range(PARTS):
+        out_ref[:, h * WIDE : (h + 1) * WIDE] = rest_v[h].astype(jnp.bfloat16)
+    for copy in spreads + asks + gives + [part for _, _, part in sums]:
         copy.wait_send()
 
 
 def local(features, weight, tiles, tile_source, tile_target, live_tiles, wanted):
     vmem = pl.BlockSpec(memory_space=pltpu.VMEM)
-    hbm = pl.BlockSpec(memory_space=pl.ANY)
+    hbm = pl.BlockSpec(memory_space=pltpu.HBM)
     smem = pl.BlockSpec(memory_space=pltpu.SMEM)
     dma = pltpu.SemaphoreType.DMA
     bf16, f32, i32 = jnp.bfloat16, jnp.float32, jnp.int32
@@ -246,15 +259,17 @@
         scratch_shapes=[
             pltpu.VMEM((BLOCK, F), bf16),
             pltpu.VMEM((F, F), bf16),
-            pltpu.VMEM((BLOCK, F), bf16),
+            pltpu.VMEM((PARTS, BLOCK, WIDE), bf16),
             pltpu.VMEM((TILES + 1, BLOCK, BLOCK), bf16),
             pltpu.VMEM((N_OFF // GROUP, NB * BLOCK, 2 * GROUP * BLOCK), bf16),
-            pltpu.VMEM((NB, BLOCK, F), bf16),
-            pltpu.VMEM((2 * N_OFF, BLOCK, F), bf16),
-            pltpu.VMEM((N_OFF, 2, BLOCK, F), bf16),
-            pltpu.VMEM((NB * BLOCK, F), f32),
-            pltpu.VMEM((NB, BLOCK, F), bf16),
-            pltpu.VMEM((NB, BLOCK, F), bf16),
+            pltpu.VMEM((NB, BLOCK, WIDE), bf16),
+            pltpu.VMEM((NB, BLOCK, WIDE), bf16),
+            pltpu.VMEM((PARTS, 2 * N_OFF, BLOCK, WIDE), bf16),
+            pltpu.VMEM((PARTS, N_OFF, 2, BLOCK, WIDE), bf16),
+            pltpu.VMEM((NB * BLOCK, WIDE), f32),
+            pltpu.VMEM((PARTS, BLOCK, WIDE), f32),
+            pltpu.VMEM((PARTS, NB, BLOCK, WIDE), bf16),
+            pltpu.VMEM((PARTS, NB, BLOCK, WIDE), bf16),
             pltpu.VMEM((1, TILES), i32),
             pltpu.VMEM((1, TILES), i32),
             pltpu.VMEM((1, SLABS), i32),
@@ -264,17 +279,23 @@
             pltpu.SMEM((2 * N_OFF, 1, 128), i32),
             pltpu.SMEM((1, NB * SLABS), i32),
             dma((6,)), dma((3,)),
-            dma((NB,)), dma((NB,)),
+            dma((PARTS, NB)), dma((PARTS, NB)),
             dma((2 * N_OFF,)), dma((2 * N_OFF,)),
-            dma((2 * N_OFF,)), dma((2 * N_OFF,)),
-            dma((NB,)), dma((NB,)),
+            dma((PARTS, 2 * N_OFF)), dma((PARTS, 2 * N_OFF)),
+            dma((PARTS, NB)), dma((PARTS, NB)),
         ],
         compiler_params=pltpu.CompilerParams(
-            collective_id=0, has_side_effects=True, vmem_limit_bytes=63 << 20
+            collective_id=0, has_side_effects=True, vmem_limit_bytes=40 << 20
         ),
     )(
-        live_tiles, features, weight, tiles,
-        tile_source.reshape(1, TILES), tile_target.reshape(1, TILES), wanted.reshape(1, SLABS),
+        live_tiles,
+        *(
+            pltpu.with_memory_space_constraint(operand, pltpu.HBM)
+            for operand in (
+                features, weight, tiles,
+                tile_source.reshape(1, TILES), tile_target.reshape(1, TILES), wanted.reshape(1, SLABS),
+            )
+        ),
     )
 
 

time: 58.8 us -> 53.3 us (0.906)
  the two profiles are of different devices: /device:TPU:1 before, /device:TPU:59 now
where the time goes in v3:
time: 53.3 us
  Pallas kernels  52 us (98%)
  between operations  0.66 us (1%)
  local copies, waits for them, and re-layouts  0.63 us (1%)
    pallas_call x1, Pallas kernels, local(): pl.pallas_call(kernel, out_shape=jax.ShapeDtypeStruct((BLOCK, F), bf16),...  52 us

profile of v3, /device:TPU:59, one launch (start us, length us, event | category | flops | bytes accessed | tf_op | source)
XLA Modules:
  0.0 53.3 jit_solution(57702849051961714)
XLA Ops:
  0.7 52.0 %shard_map.73 = bf16[128,256]{1,0:T(8,128)(2,1)S(1)} custom-call(s32[1,1]{1,0:T(1,128)S(6)} %copy.9.live_ref, bf16[128,256]{1,0:T(8,128)(2,1)} %features_ref.1, bf16[256,256]{1,0:T(8,128)(2,1)} %weight_ref.1, bf16[1,1,128,128,128]{4,3,2,1,0:T(8,128)(2,1)} %tiles_ref.1, s32[1,128]{1,0:T(1,128)} %bitcast.3, s32[1,128]{1,0:T(1,128)} %bitcast.4, s32[1,32]{1,0:T(1,128)} %bitcast.5), custom_call_target="tpu_custom_call" | custom-call | tf_op jit(solution)/shard_map/pallas_call | solution.py:254
  52.6 0.6 %copy.10 = bf16[128,256]{1,0:T(8,128)(2,1)} copy(bf16[128,256]{1,0:T(8,128)(2,1)S(1)} %shard_map.73) | data formatting | bytes 131072

commit v4 on v3

--- a/solution.py
+++ b/solution.py
@@ -12,13 +12,13 @@
 NB = 8
 TILES = 128
 SLABS = 32
-GROUP = 4
+GROUP = 16
 MESH = pl.DeviceIdType.MESH
 
 OFFSETS = [
-    (2, 0, 0), (0, 2, 0), (1, 1, 0), (3, 3, 0),
-    (1, 3, 0), (3, 1, 0), (1, 0, 1), (3, 0, 1),
-    (0, 1, 1), (0, 3, 1), (0, 0, 1), (1, 0, 0),
+    (1, 0, 1), (3, 0, 1), (0, 1, 1), (0, 3, 1),
+    (0, 0, 1), (2, 0, 0), (0, 2, 0), (1, 1, 0),
+    (3, 3, 0), (1, 3, 0), (3, 1, 0), (1, 0, 0),
     (3, 0, 0), (0, 1, 0), (0, 3, 0), (0, 0, 0),
 ]
 HOME = OFFSETS.index((0, 0, 0))
@@ -236,13 +236,15 @@
                 sums.append((h, d, part))
             else:
                 rest_v[h] = full
+    for copy in spreads + asks + gives:
+        copy.wait_send()
     for h, d, part in sums:
         part.wait_recv()
         rest_v[h] += land_v[h, d].astype(jnp.float32)
     for h in range(PARTS):
         out_ref[:, h * WIDE : (h + 1) * WIDE] = rest_v[h].astype(jnp.bfloat16)
-    for copy in spreads + asks + gives + [part for _, _, part in sums]:
-        copy.wait_send()
+    for _, _, part in sums:
+        part.wait_send()
 
 
 def local(features, weight, tiles, tile_source, tile_target, live_tiles, wanted):

time: 53.3 us -> 52.3 us (0.981)
  the two profiles are of different devices: /device:TPU:59 before, /device:TPU:33 now
where the time goes in v4:
time: 52.3 us; the launch traced here: 52.2 us
  Pallas kernels  50.9 us (97%)
  between operations  0.66 us (1%)
  local copies, waits for them, and re-layouts  0.63 us (1%)
    pallas_call x1, Pallas kernels, local(): pl.pallas_call(kernel, out_shape=jax.ShapeDtypeStruct((BLOCK, F), bf16),...  50.9 us

profile of v4, /device:TPU:33, one launch (start us, length us, event | category | flops | bytes accessed | tf_op | source)
XLA Modules:
  0.0 52.2 jit_solution(1981279648319739984)
XLA Ops:
  0.7 50.9 %shard_map.73 = bf16[128,256]{1,0:T(8,128)(2,1)S(1)} custom-call(s32[1,1]{1,0:T(1,128)S(6)} %copy.9.live_ref, bf16[128,256]{1,0:T(8,128)(2,1)} %features_ref.1, bf16[256,256]{1,0:T(8,128)(2,1)} %weight_ref.1, bf16[1,1,128,128,128]{4,3,2,1,0:T(8,128)(2,1)} %tiles_ref.1, s32[1,128]{1,0:T(1,128)} %bitcast.3, s32[1,128]{1,0:T(1,128)} %bitcast.4, s32[1,32]{1,0:T(1,128)} %bitcast.5), custom_call_target="tpu_custom_call" | custom-call | tf_op jit(solution)/shard_map/pallas_call | solution.py:256
  51.6 0.6 %copy.10 = bf16[128,256]{1,0:T(8,128)(2,1)} copy(bf16[128,256]{1,0:T(8,128)(2,1)S(1)} %shard_map.73) | data formatting | bytes 131072

commit v5 on v4

--- a/solution.py
+++ b/solution.py
@@ -47,7 +47,7 @@
 
 def kernel(
     live_ref, features_ref, weight_ref, tiles_ref, source_ref, target_ref, wanted_ref, out_ref,
-    feat_v, weight_v, hidden_v, tiles_v, dense_v, slab_0_v, slab_1_v, picked_v, panel_v, total_v, rest_v, part_v, land_v,
+    feat_v, weight_v, hidden_v, tiles_v, dense_v, slab_0_v, slab_1_v, picked_v, panel_v, rest_v, part_v, land_v,
     source_v, target_v, wanted_v, ask_v, req_v, slot_v, req_s, slot_s,
     load_sem, small_sem, spread_send, spread_recv, ask_send, ask_recv, give_send, give_recv, sum_send, sum_recv,
 ):
@@ -110,7 +110,7 @@
     spreads = []
 
     def spread_part(h):
-        for dz in (0, 1, 7, 2, 6, 3, 5, 4):
+        for dz in (0, 1, 7, 2, 6, 3, 5, 4) if h == 0 else (4, 3, 5, 2, 6, 1, 7, 0):
             spread = pltpu.make_async_remote_copy(
                 src_ref=hidden_v.at[h], dst_ref=slabs_v[h].at[q], send_sem=spread_send.at[h, dz], recv_sem=spread_recv.at[h, q],
                 device_id=owner_at(z, yh, c, lax.rem(z + dz, 8)), device_id_type=MESH,
@@ -205,37 +205,28 @@
     def panels(h, g):
         return panel_v[h, g * GROUP : (g + 1) * GROUP].reshape(2 * GROUP * BLOCK, WIDE)
 
-    ROWS = 256
     last = N_OFF // GROUP - 1
     sums = []
     for h in range(PARTS):
-        for g in range(last):
-            arrive(h, g)
-
-            @pl.loop(0, NB * BLOCK // ROWS)
-            def _(i):
-                at = pl.ds(pl.multiple_of(i * ROWS, ROWS), ROWS)
-                term = jnp.dot(dense_v[g, at, :], panels(h, g), preferred_element_type=jnp.float32)
-                if g == 0:
-                    total_v[at, :] = term
-                else:
-                    total_v[at, :] += term
-
         arrive(h, last)
-        for d in range(1, NB + 1):
-            b = lax.rem(q + d, NB)
+
+        def full(b):
             at = pl.ds(pl.multiple_of(b * BLOCK, BLOCK), BLOCK)
-            full = total_v[at, :] + jnp.dot(dense_v[last, at, :], panels(h, last), preferred_element_type=jnp.float32)
-            if d < NB:
-                part_v[h, d] = full.astype(jnp.bfloat16)
-                part = pltpu.make_async_remote_copy(
-                    src_ref=part_v.at[h, d], dst_ref=land_v.at[h, d], send_sem=sum_send.at[h, d], recv_sem=sum_recv.at[h, d],
-                    device_id=(r, b), device_id_type=MESH,
-                )
-                part.start()
-                sums.append((h, d, part))
-            else:
-                rest_v[h] = full
+            return jnp.dot(dense_v[0, at, :], panels(h, 0), preferred_element_type=jnp.float32)
+
+        def part_to(d, h=h):
+            return pltpu.make_async_remote_copy(
+                src_ref=part_v.at[h, d], dst_ref=land_v.at[h, d], send_sem=sum_send.at[h, d], recv_sem=sum_recv.at[h, d],
+                device_id=(r, lax.rem(q + d, NB)), device_id_type=MESH,
+            )
+
+        @pl.loop(1, NB)
+        def _(d):
+            part_v[h, d] = full(lax.rem(q + d, NB)).astype(jnp.bfloat16)
+            part_to(d).start()
+
+        rest_v[h] = full(q)
+        sums += [(h, d, part_to(d)) for d in range(1, NB)]
     for copy in spreads + asks + gives:
         copy.wait_send()
     for h, d, part in sums:
@@ -268,7 +259,6 @@
             pltpu.VMEM((NB, BLOCK, WIDE), bf16),
             pltpu.VMEM((PARTS, 2 * N_OFF, BLOCK, WIDE), bf16),
             pltpu.VMEM((PARTS, N_OFF, 2, BLOCK, WIDE), bf16),
-            pltpu.VMEM((NB * BLOCK, WIDE), f32),
             pltpu.VMEM((PARTS, BLOCK, WIDE), f32),
             pltpu.VMEM((PARTS, NB, BLOCK, WIDE), bf16),
             pltpu.VMEM((PARTS, NB, BLOCK, WIDE), bf16),

time: 52.3 us -> 51.4 us (0.983)
  the two profiles are of different devices: /device:TPU:33 before, /device:TPU:1 now
where the time goes in v5:
time: 51.4 us; the launch traced here: 51.3 us
  Pallas kernels  50 us (97%)
  between operations  0.66 us (1%)
  local copies, waits for them, and re-layouts  0.63 us (1%)
    pallas_call x1, Pallas kernels, local(): pl.pallas_call(kernel, out_shape=jax.ShapeDtypeStruct((BLOCK, F), bf16),...  50 us

profile of v5, /device:TPU:1, one launch (start us, length us, event | category | flops | bytes accessed | tf_op | source)
XLA Modules:
  0.0 51.3 jit_solution(8577467000932752669)
XLA Ops:
  0.7 50.0 %shard_map.73 = bf16[128,256]{1,0:T(8,128)(2,1)S(1)} custom-call(s32[1,1]{1,0:T(1,128)S(6)} %copy.9.live_ref, bf16[128,256]{1,0:T(8,128)(2,1)} %features_ref.1, bf16[256,256]{1,0:T(8,128)(2,1)} %weight_ref.1, bf16[1,1,128,128,128]{4,3,2,1,0:T(8,128)(2,1)} %tiles_ref.1, s32[1,128]{1,0:T(1,128)} %bitcast.3, s32[1,128]{1,0:T(1,128)} %bitcast.4, s32[1,32]{1,0:T(1,128)} %bitcast.5), custom_call_target="tpu_custom_call" | custom-call | tf_op jit(solution)/shard_map/pallas_call | solution.py:247
  50.7 0.6 %copy.10 = bf16[128,256]{1,0:T(8,128)(2,1)} copy(bf16[128,256]{1,0:T(8,128)(2,1)S(1)} %shard_map.73) | data formatting | bytes 131072

commit v6 on v5

--- a/solution.py
+++ b/solution.py
@@ -109,8 +109,8 @@
 
     spreads = []
 
-    def spread_part(h):
-        for dz in (0, 1, 7, 2, 6, 3, 5, 4) if h == 0 else (4, 3, 5, 2, 6, 1, 7, 0):
+    def spread_part(h, order=(4, 3, 5, 2, 6, 1, 7, 0)):
+        for dz in order:
             spread = pltpu.make_async_remote_copy(
                 src_ref=hidden_v.at[h], dst_ref=slabs_v[h].at[q], send_sem=spread_send.at[h, dz], recv_sem=spread_recv.at[h, q],
                 device_id=owner_at(z, yh, c, lax.rem(z + dz, 8)), device_id_type=MESH,
@@ -118,7 +118,7 @@
             spread.start()
             spreads.append(spread)
 
-    spread_part(0)
+    spread_part(0, (0, 1, 7, 4))
     asks = []
     for k in range(N_OFF):
         for core in (1 - c,) if k == HOME else (0, 1):
@@ -128,6 +128,7 @@
             )
             ask.start()
             asks.append(ask)
+    spread_part(0, (2, 6, 3, 5))
     for h in range(1, PARTS):
         spread_part(h)
     mine = pltpu.make_async_copy(ask_v, req_v.at[2 * HOME + c], small_sem.at[0])

time: 51.4 us -> 51.5 us (level)
  no operation moved by 1% of the time
where the time goes in v6:
time: 51.5 us; the launch traced here: 51.2 us
  Pallas kernels  49.9 us (97%)
  between operations  0.66 us (1%)
  local copies, waits for them, and re-layouts  0.63 us (1%)
    pallas_call x1, Pallas kernels, local(): pl.pallas_call(kernel, out_shape=jax.ShapeDtypeStruct((BLOCK, F), bf16),...  49.9 us

profile of v6, /device:TPU:1, one launch (start us, length us, event | category | flops | bytes accessed | tf_op | source)
XLA Modules:
  0.0 51.2 jit_solution(550347366330593047)
XLA Ops:
  0.7 49.9 %shard_map.73 = bf16[128,256]{1,0:T(8,128)(2,1)S(1)} custom-call(s32[1,1]{1,0:T(1,128)S(6)} %copy.9.live_ref, bf16[128,256]{1,0:T(8,128)(2,1)} %features_ref.1, bf16[256,256]{1,0:T(8,128)(2,1)} %weight_ref.1, bf16[1,1,128,128,128]{4,3,2,1,0:T(8,128)(2,1)} %tiles_ref.1, s32[1,128]{1,0:T(1,128)} %bitcast.3, s32[1,128]{1,0:T(1,128)} %bitcast.4, s32[1,32]{1,0:T(1,128)} %bitcast.5), custom_call_target="tpu_custom_call" | custom-call | tf_op jit(solution)/shard_map/pallas_call | solution.py:248
  50.6 0.6 %copy.10 = bf16[128,256]{1,0:T(8,128)(2,1)} copy(bf16[128,256]{1,0:T(8,128)(2,1)S(1)} %shard_map.73) | data formatting | bytes 131072
